TPU v7x, 256 devices: a whole 4x4x8 slice. The times are simulated.
256 devices in a mesh: section: 16 (over z, x_hi), tensor: 16 (over x_lo, y, core).
Axes of the slice: x: 4 (x_hi: 2, x_lo: 2; x = x_hi * 2 + x_lo), y: 4, z: 8, core: 2. Of those that a mesh axis runs over, the one named last changes fastest.
Arguments:
- handed_state: bfloat16 [16, 2, 512, 4096], P('section', None, 'tensor'), may hold values from -6 to 6
- handed_grad: bfloat16 [16, 2, 512, 4096], P('section', None, 'tensor'), may hold values from -6 to 6
- top_state: bfloat16 [2, 512, 4096], P(None, 'tensor'), may hold values from -6 to 6
- loss_grad: bfloat16 [2, 512, 4096], P(None, 'tensor'), may hold values from -6 to 6
- ln_gain: bfloat16 [16, 4096], P('section'), may hold values from 0.099609375 to 1.8984375
- w_qkv: bfloat16 [16, 3, 4096, 4096], P('section', None, None, 'tensor'), may hold values from -0.09375 to 0.09375
- w_out: bfloat16 [16, 4096, 4096], P('section', 'tensor'), may hold values from -0.375 to 0.375
Outputs:
- rebuilt: bfloat16 [16, 2, 512, 4096], P('section', None, 'tensor')
- input_grad: bfloat16 [16, 2, 512, 4096], P('section', None, 'tensor')
All inputs are finite; a program needn't handle non-finite values.
Results may differ from a plain program's by a relative error of at most 0.018.
Values may be sent and summed in bfloat16 or wider, within the bound.
A program may use at most 64 MiB of HBM per device.

v0:
```python
import jax
import jax.numpy as jnp
from jax import lax
from jax.sharding import PartitionSpec as P

HD = 128
TOK = 256


def shifted(array, axis, by):
    count = lax.axis_size(axis)
    pairs = [(i, i + by) for i in range(count) if 0 <= i + by < count]
    return lax.ppermute(array, axis, pairs)


def normalize(rows, norm_gain):
    values = rows.astype(jnp.float32)
    row_mean = jnp.mean(values, axis=-1, keepdims=True)
    centred = values - row_mean
    inv_scale = lax.rsqrt(jnp.mean(centred * centred, axis=-1, keepdims=True) + 1e-06)
    unit_rows = centred * inv_scale
    return ((unit_rows * norm_gain.astype(jnp.float32)).astype(jnp.bfloat16), unit_rows, inv_scale)


def unit_norm(values):
    row_mean = jnp.mean(values, axis=-1, keepdims=True)
    centred = values - row_mean
    inv_scale = lax.rsqrt(jnp.mean(centred * centred, axis=-1, keepdims=True) + 1e-06)
    return (centred * inv_scale, inv_scale)


def norm_back(grad_unit, unit_rows, inv_scale):
    first_mean = jnp.mean(grad_unit, axis=-1, keepdims=True)
    second_mean = jnp.mean(grad_unit * unit_rows, axis=-1, keepdims=True)
    return (grad_unit - first_mean - unit_rows * second_mean) * inv_scale


def core_forward(query_raw, key_raw, value_rows):
    query_unit, query_scale = unit_norm(query_raw)
    key_unit, key_scale = unit_norm(key_raw)
    query_half = query_unit.astype(jnp.bfloat16)
    key_half = key_unit.astype(jnp.bfloat16)
    scores = jnp.einsum(
        "iqhc,ikhc->ihqk", query_half, key_half, preferred_element_type=jnp.float32
    ) * HD ** (-0.5)
    exponent = jnp.exp(scores)
    attn_prob = exponent / jnp.sum(exponent, axis=-1, keepdims=True)
    prob_half = attn_prob.astype(jnp.bfloat16)
    mixed = jnp.einsum(
        "ihqk,ikhc->iqhc", prob_half, value_rows, preferred_element_type=jnp.float32
    ).astype(jnp.bfloat16)
    return (
        mixed,
        (query_unit, query_scale, key_unit, key_scale, query_half, key_half, attn_prob, prob_half),
    )


def core_backward(mixed_grad, value_rows, saved):
    query_unit, query_scale, key_unit, key_scale, query_half, key_half, attn_prob, prob_half = saved
    prob_grad = jnp.einsum(
        "iqhc,ikhc->ihqk", mixed_grad, value_rows, preferred_element_type=jnp.float32
    )
    value_grad = jnp.einsum(
        "ihqk,iqhc->ikhc", prob_half, mixed_grad, preferred_element_type=jnp.float32
    ).astype(jnp.bfloat16)
    inner = jnp.sum(prob_grad * attn_prob, axis=-1, keepdims=True)
    score_grad = (attn_prob * (prob_grad - inner) * HD ** (-0.5)).astype(jnp.bfloat16)
    query_part = jnp.einsum(
        "ihqk,ikhc->iqhc", score_grad, key_half, preferred_element_type=jnp.float32
    )
    key_part = jnp.einsum(
        "ihqk,iqhc->ikhc", score_grad, query_half, preferred_element_type=jnp.float32
    )
    query_grad = norm_back(query_part, query_unit, query_scale).astype(jnp.bfloat16)
    key_grad = norm_back(key_part, key_unit, key_scale).astype(jnp.bfloat16)
    return (query_grad, key_grad, value_grad)


def on_device(handed_state, handed_grad, top_state, loss_grad, ln_gain, w_qkv, w_out):
    norm_gain = ln_gain[0]
    weights = w_qkv[0]
    out_weights = w_out[0]
    local_rows = handed_state.shape[2]
    section_index = lax.axis_index("section")
    last_section = lax.axis_size("section") - 1
    returned_state, returned_grad = shifted((handed_state[0], handed_grad[0]), "section", -1)
    state_now = jnp.where(section_index == last_section, top_state, returned_state)
    grad_now = jnp.where(section_index == last_section, loss_grad, returned_grad)
    first_out = state_now[0]
    second_out = state_now[1]
    first_grad = grad_now[0]
    second_grad = grad_now[1]
    normed, unit_rows, inv_scale = normalize(first_out, norm_gain)
    projected = jnp.einsum(
        "td,kdc->tkc",
        lax.all_gather(normed, "tensor", axis=0, tiled=True),
        weights,
        preferred_element_type=jnp.float32,
    )
    grad_all = lax.all_gather(second_grad, "tensor", axis=0, tiled=True)
    tokens = projected.shape[0]
    images = tokens // TOK
    local_heads = projected.shape[2] // HD
    query_raw = projected[:, 0].reshape(images, TOK, local_heads, HD)
    key_raw = projected[:, 1].reshape(images, TOK, local_heads, HD)
    value_rows = projected[:, 2].astype(jnp.bfloat16).reshape(images, TOK, local_heads, HD)
    mixed, saved = core_forward(query_raw, key_raw, value_rows)
    mixed, value_rows, saved = (mixed.reshape(tokens, local_heads * HD), value_rows, saved)
    tokens = mixed.shape[0]
    images = tokens // TOK
    local_heads = value_rows.shape[2]
    rows = mixed
    head_total = lax.psum_scatter(
        jnp.dot(rows, out_weights, preferred_element_type=jnp.float32).astype(jnp.bfloat16),
        "tensor",
        scatter_dimension=0,
        tiled=True,
    ).astype(jnp.float32)
    mixed_grad = jnp.einsum("td,cd->tc", grad_all, out_weights, preferred_element_type=jnp.float32)
    mixed_grad = mixed_grad.astype(jnp.bfloat16).reshape(images, TOK, local_heads, HD)
    query_grad, key_grad, value_grad = core_backward(mixed_grad, value_rows, saved)
    flat_grads = (
        query_grad.reshape(tokens, -1),
        key_grad.reshape(tokens, -1),
        value_grad.reshape(tokens, -1),
    )
    summed = jnp.zeros((lax.axis_size("tensor") * local_rows, weights.shape[1]), jnp.float32)
    for member in range(3):
        rows = flat_grads[member]
        summed = summed + jnp.einsum(
            "tc,dc->td", rows, weights[member], preferred_element_type=jnp.float32
        )
    normed_grad = lax.psum_scatter(
        summed.astype(jnp.bfloat16), "tensor", scatter_dimension=0, tiled=True
    ).astype(jnp.float32)
    first_in = (second_out.astype(jnp.float32) - head_total).astype(jnp.bfloat16)
    input_part = norm_back(normed_grad * norm_gain.astype(jnp.float32), unit_rows, inv_scale)
    second_in_grad = (first_grad.astype(jnp.float32) + input_part).astype(jnp.bfloat16)
    rebuilt_now = jnp.stack([first_in, first_out])
    grads_now = jnp.stack([second_grad, second_in_grad])
    return (rebuilt_now[None], grads_now[None])


def solution(mesh):
    placed = (
        P("section", None, "tensor", None),
        P("section", None, "tensor", None),
        P(None, "tensor", None),
        P(None, "tensor", None),
        P("section", None),
        P("section", None, None, "tensor"),
        P("section", "tensor", None),
    )
    return jax.shard_map(
        on_device,
        mesh=mesh,
        in_specs=placed,
        out_specs=(P("section", None, "tensor", None), P("section", None, "tensor", None)),
        check_vma=False,
    )
```

profile of v0, /device:TPU:4, one launch (start us, length us, event | category | flops | bytes accessed | tf_op | source)
XLA Modules:
  0.0 301.2 jit_solution(4786781107959393325)
XLA Ops:
  7.2 0.0 all-gather.4.cloned.1.call-start
  7.2 4.3 %collective-permute-start = (bf16[2,32,4096]{2,1,0:T(8,128)(2,1)}, bf16[2,32,4096]{2,1,0:T(8,128)(2,1)S(1)}, u32[]{:S(2)}, u32[]{:S(2)}) collective-permute-start(bf16[2,32,4096]{2,1,0:T(8,128)(2,1)} %bitcast.129), channel_id=1, source_target_pairs={{16,0},{32,16},{48,32},{64,48},{80,64},{96,80},{112,96},{128,112},... | collective-permute-start | bytes 1572872 | tf_op jit(solution)/shard_map/ppermute | solution.py:13
  11.5 0.7 mul.153
  12.3 13.3 %collective-permute-done = bf16[2,32,4096]{2,1,0:T(8,128)(2,1)S(1)} collective-permute-done((bf16[2,32,4096]{2,1,0:T(8,128)(2,1)}, bf16[2,32,4096]{2,1,0:T(8,128)(2,1)S(1)}, u32[]{:S(2)}, u32[]{:S(2)}) %collective-permute-start) | collective-permute-done | bytes 524320 | tf_op jit(solution)/shard_map/ppermute | solution.py:13
  25.5 0.1 broadcast_select_fusion.1
  25.6 0.2 convert_reduce_fusion
  25.7 0.3 fusion.44
  26.0 0.9 fusion.38
  26.9 0.0 all-gather.4.cloned.1.call-update
  26.9 0.0 all-gather.6.cloned.1.call-start
  26.9 1.9 collective-permute-start.1
  28.9 15.5 %collective-permute-done.1 = bf16[2,32,4096]{2,1,0:T(8,128)(2,1)S(1)} collective-permute-done((bf16[2,32,4096]{2,1,0:T(8,128)(2,1)}, bf16[2,32,4096]{2,1,0:T(8,128)(2,1)S(1)}, u32[]{:S(2)}, u32[]{:S(2)}) %collective-permute-start.1) | collective-permute-done | bytes 524320 | tf_op jit(solution)/shard_map/ppermute | solution.py:13
  44.4 0.1 broadcast_select_fusion
  44.4 0.8 copy-done.2
  45.3 0.7 slice.49
  46.0 0.0 all-gather.6.cloned.1.call-update
  46.0 0.0 reduce-scatter.5.cloned.1.call-start
  46.1 23.5 %all-gather.4.cloned.1.call-done = bf16[512,4096]{1,0:T(8,128)(2,1)} async-done(((bf16[32,4096]{1,0:T(8,128)(2,1)}), bf16[512,4096]{1,0:T(8,128)(2,1)}) %all-gather.4.cloned.1.call-update) | async-done | bytes 4194320 | tf_op jit(solution)/shard_map/all_gather | solution.py:96
  69.6 7.0 %fusion.1 = f32[512,3,256]{2,0,1:T(8,128)S(1)} fusion(bf16[1,3,4096,256]{3,2,1,0:T(8,128)(2,1)} %param.12, bf16[512,4096]{1,0:T(8,128)(2,1)} %all-gather.4.cloned.1.call-done), kind=kOutput, calls=%fused_computation.2 | convolution fusion | flops 3221225472 | bytes 12058624 | tf_op jit(solution)/shard_map/td,kdc->tkc/dot_general | solution.py:94
  76.7 0.9 fusion.77
  77.5 1.1 reshape_squeeze.7
  78.6 1.2 copy.90
  79.8 2.4 reduce_sum.130
  82.2 2.1 reshape_squeeze.6
  84.3 2.4 reduce_sum.128
  86.7 2.0 copy.88
  88.7 0.8 convert_element_type.85
  89.5 1.1 copy.89
  90.5 1.1 copy.87
  91.6 0.1 multiply_reduce_fusion.3
  91.7 1.1 multiply_reduce_fusion.4
  92.9 19.5 %all-gather.6.cloned.1.call-done = bf16[1,512,4096]{2,1,0:T(8,128)(2,1)} async-done(((bf16[1,32,4096]{2,1,0:T(8,128)(2,1)}), bf16[1,512,4096]{2,1,0:T(8,128)(2,1)}) %all-gather.6.cloned.1.call-update) | async-done | bytes 4194320 | tf_op jit(solution)/shard_map/all_gather | solution.py:100
  112.4 4.2 %fusion.21 = bf16[512,256]{1,0:T(8,128)(2,1)} fusion(bf16[1,256,4096]{2,1,0:T(8,128)(2,1)S(1)} %copy-done, bf16[1,512,4096]{2,1,0:T(8,128)(2,1)} %all-gather.6.cloned.1.call-done), kind=kOutput, calls=%fused_computation.26 | convolution fusion | flops 1073872896 | bytes 6553600 | tf_op jit(solution)/shard_map/td,cd->tc/dot_general | solution.py:119
  116.5 1.0 reshape.104
  117.6 0.8 copy.102
  118.4 1.9 fusion.51
  120.3 2.3 fusion.66
  122.6 2.4 fusion.48
  125.0 3.6 %fusion.76 = (f32[2,256,2]{1,2,0:T(2,128)S(1)}, f32[2,256,2]{1,2,0:T(2,128)S(1)}, f32[2,256,2,128]{1,3,2,0:T(8,128)}) fusion(f32[2,256,2]{1,2,0:T(2,128)S(1)} %add_rsqrt_fusion.1, f32[2,256,2,128]{1,3,2,0:T(8,128)} %copy.88, f32[2,256,2]{1,2,0:T(2,128)S(1)} %broadcast_multiply_fusion.5, bf16[2,256,2,128]{1,3,2,0:T(8,128)(2,1)} %get-tuple-element.15, ...), kind=kOutput, calls=%fused_computation.109 | convolution fusion | flops 69074176 | bytes 3424256 | tf_op jit(solution)/shard_map/ihqk,ikhc->iqhc/dot_general | solution.py:68
  128.6 3.4 %fusion.75 = (f32[2,256,2]{1,2,0:T(2,128)S(1)}, f32[2,256,2]{1,2,0:T(2,128)S(1)}, f32[2,256,2,128]{1,3,2,0:T(8,128)}) fusion(f32[2,256,2]{1,2,0:T(2,128)S(1)} %add_rsqrt_fusion, f32[2,256,2,128]{1,3,2,0:T(8,128)S(1)} %copy.90, f32[2,256,2]{1,2,0:T(2,128)S(1)} %broadcast_multiply_fusion.4, bf16[2,256,2,128]{1,3,2,0:T(8,128)(2,1)S(1)} %get-tuple-element.14, ...), kind=kOutput, calls=%fused_computation.108 | convolution fusion | flops 69074176 | bytes 3424256 | tf_op jit(solution)/shard_map/ihqk,iqhc->ikhc/dot_general | solution.py:71
  132.0 2.3 fusion.19
  134.3 1.3 multiply_convert_fusion.1
  135.7 0.9 copy.99
  136.5 1.2 multiply_convert_fusion
  137.7 0.2 copy.101
  137.9 2.0 fusion.27
  139.9 0.2 copy.104
  140.0 2.9 fusion.7
  143.0 2.9 fusion.9
  145.9 5.0 %add_convert_fusion = bf16[512,4096]{1,0:T(8,128)(2,1)} fusion(f32[512,4096]{1,0:T(8,128)S(1)} %fusion.9, f32[512,4096]{1,0:T(8,128)S(1)} %fusion.7, bf16[1,3,4096,256]{3,2,1,0:T(8,128)(2,1)} %param.12, bf16[64,8,2,128]{3,2,1,0:T(2,128)(2,1)S(1)} %bitcast.122), kind=kOutput, calls=%fused_computation.1 | convolution fusion | flops 1080033280 | bytes 23330816 | tf_op jit(solution)/shard_map/tc,dc->td/dot_general | solution.py:130
  150.8 0.0 reduce-scatter.5.cloned.1.call-update
  150.9 0.2 reduce-scatter.3.cloned.1.call-start
  151.1 0.7 copy-done.4
  151.8 1.9 fusion.26
  153.7 0.2 copy.95
  153.8 3.2 %convolution_convert_fusion = bf16[512,4096]{1,0:T(8,128)(2,1)} fusion(bf16[1,256,4096]{2,1,0:T(8,128)(2,1)S(1)} %copy-done, bf16[64,8,2,128]{3,2,1,0:T(2,128)(2,1)S(1)} %bitcast.123), kind=kOutput, calls=%fused_computation.4 | convolution fusion | flops 1075838976 | bytes 6553600 | tf_op jit(solution)/shard_map/dot_general | solution.py:114
  157.1 0.0 reduce-scatter.3.cloned.1.call-update
  157.1 0.7 slice.45
  157.8 62.7 %reduce-scatter.5.cloned.1.call-done = bf16[32,4096]{1,0:T(8,128)(2,1)} async-done(((bf16[512,4096]{1,0:T(8,128)(2,1)}), bf16[32,4096]{1,0:T(8,128)(2,1)}) %reduce-scatter.5.cloned.1.call-update) | async-done | bytes 262160 | tf_op jit(solution)/shard_map/reduce_scatter | solution.py:133
  220.5 1.2 fusion.46
  221.7 69.0 %reduce-scatter.3.cloned.1.call-done = bf16[32,4096]{1,0:T(8,128)(2,1)} async-done(((bf16[512,4096]{1,0:T(8,128)(2,1)}), bf16[32,4096]{1,0:T(8,128)(2,1)}) %reduce-scatter.3.cloned.1.call-update) | async-done | bytes 262160 | tf_op jit(solution)/shard_map/reduce_scatter | solution.py:113
  290.8 1.3 fusion.54
  292.1 0.8 maximum_bitcast_fusion.1
  292.9 1.8 maximum_bitcast_fusion
  (23 shorter events, 0.1 us)
Async XLA Ops:
  7.2 105.2 %copy-start = (bf16[1,256,4096]{2,1,0:T(8,128)(2,1)S(1)}, bf16[1,256,4096]{2,1,0:T(8,128)(2,1)}, u32[]{:S(2)}) copy-start(bf16[1,256,4096]{2,1,0:T(8,128)(2,1)} %param.13) | copy-start | bytes 6291460
  7.2 62.4 %all-gather.4.cloned.1.call-start = ((), (), s32[]{:S(2)}) async-start(), calls=%async_computation.2 | async-start | bytes 4456448 | tf_op jit(solution)/shard_map/all_gather | solution.py:96
  7.2 18.3 %collective-permute-start = (bf16[2,32,4096]{2,1,0:T(8,128)(2,1)}, bf16[2,32,4096]{2,1,0:T(8,128)(2,1)S(1)}, u32[]{:S(2)}, u32[]{:S(2)}) collective-permute-start(bf16[2,32,4096]{2,1,0:T(8,128)(2,1)} %bitcast.129), channel_id=1, source_target_pairs={{16,0},{32,16},{48,32},{64,48},{80,64},{96,80},{112,96},{128,112},... | collective-permute-start | bytes 1572872 | tf_op jit(solution)/shard_map/ppermute | solution.py:13
  26.9 85.5 %all-gather.6.cloned.1.call-start = ((), (), s32[]{:S(2)}) async-start(), calls=%async_computation.5 | async-start | bytes 4456448 | tf_op jit(solution)/shard_map/all_gather | solution.py:100
  26.9 17.4 %collective-permute-start.1 = (bf16[2,32,4096]{2,1,0:T(8,128)(2,1)}, bf16[2,32,4096]{2,1,0:T(8,128)(2,1)S(1)}, u32[]{:S(2)}, u32[]{:S(2)}) collective-permute-start(bf16[2,32,4096]{2,1,0:T(8,128)(2,1)} %bitcast.130), channel_id=1, source_target_pairs={{16,0},{32,16},{48,32},{64,48},{80,64},{96,80},{112,96},{128,112},... | collective-permute-start | bytes 1572872 | tf_op jit(solution)/shard_map/ppermute | solution.py:13
  44.4 0.8 copy-start.2
  46.0 174.4 %reduce-scatter.5.cloned.1.call-start = ((), (), s32[]{:S(2)}) async-start(), calls=%async_computation.4 | async-start | bytes 4456448 | tf_op jit(solution)/shard_map/reduce_scatter | solution.py:133
  140.0 2.9 copy-start.5
  150.8 0.9 copy-start.4
  150.9 139.9 %reduce-scatter.3.cloned.1.call-start = ((), (), s32[]{:S(2)}) async-start(), calls=%async_computation.3 | async-start | bytes 4456448 | tf_op jit(solution)/shard_map/reduce_scatter | solution.py:113
  157.1 133.7 %copy-start.3 = (bf16[2,32,4096]{2,1,0:T(8,128)(2,1)S(1)}, bf16[2,32,4096]{2,1,0:T(8,128)(2,1)}, u32[]{:S(2)}) copy-start(bf16[2,32,4096]{2,1,0:T(8,128)(2,1)} %copy-done.2) | copy-start | bytes 1572868
  157.1 135.0 %copy-start.1 = (bf16[1,32,4096]{2,1,0:T(8,128)(2,1)S(1)}, bf16[1,32,4096]{2,1,0:T(8,128)(2,1)}, u32[]{:S(2)}) copy-start(bf16[1,32,4096]{2,1,0:T(8,128)(2,1)} %slice.49) | copy-start | bytes 786436
Sparse Core Ops, SparseCore 0:
  27.0 42.5 all-gather.3
  71.5 40.8 all-gather.5
  151.0 69.4 reduce-scatter.4
  222.9 67.8 reduce-scatter.2
where the time goes:
time: 302 us; the launch traced here: 301 us
  waiting for transfers between devices  204 us (68%)
  matrix products  43.1 us (14%)
  other arithmetic  17.6 us (6%)
  local copies, waits for them, and re-layouts  16.4 us (5%)
  between operations  14 us (5%)
  starting transfers between devices  6.55 us (2%)
    reduce_scatter x1, waiting for transfers between devices, on_device(): lax.psum_scatter(jnp.dot(rows, out_weights, preferred_element_type=jnp.fl...  69 us
    reduce_scatter x1, waiting for transfers between devices, on_device(): lax.psum_scatter(summed.astype(jnp.bfloat16), 'tensor', scatter_dimension...  62.7 us
    ppermute x2, waiting for transfers between devices, shifted(): return lax.ppermute(array, axis, pairs)  28.7 us
    all_gather x1, waiting for transfers between devices, on_device(): lax.all_gather(normed, 'tensor', axis=0, tiled=True)  23.5 us
    all_gather x1, waiting for transfers between devices, on_device(): grad_all = lax.all_gather(second_grad, 'tensor', axis=0, tiled=True)  19.5 us
    dot_general x3, matrix products, on_device(): jnp.einsum('tc,dc->td', rows, weights[member], preferred_element_type=jnp...  10.8 us
    dot_general x1, matrix products, on_device(): jnp.einsum('td,kdc->tkc', lax.all_gather(normed, 'tensor', axis=0, tiled=...  7.03 us
    ppermute x2, starting transfers between devices, shifted(): return lax.ppermute(array, axis, pairs)  6.2 us
  transfers between devices with their start and end apart: 6, of which 6 were waited for; matrix products, arithmetic and copies ran while one was open for 11% of the time, Pallas kernels for 0%

commit v1 on v0

v1 whole, which is shorter than its diff:
```python
import functools

import jax
import jax.numpy as jnp
from jax import lax
from jax.experimental import pallas as pl
from jax.experimental.pallas import tpu as pltpu
from jax.sharding import PartitionSpec as P

HD = 128
MESH = pl.DeviceIdType.MESH
F32 = jnp.float32
BF16 = jnp.bfloat16
R = 32
N_COPIES = 128


def mean_last(values):
    return jnp.mean(values, axis=-1, keepdims=True)


def unit_norm(values):
    centred = values - mean_last(values)
    inv_scale = lax.rsqrt(mean_last(centred * centred) + 1e-06)
    return centred * inv_scale, inv_scale


def norm_back(grad_unit, unit_rows, inv_scale):
    first_mean = mean_last(grad_unit)
    second_mean = mean_last(grad_unit * unit_rows)
    return (grad_unit - first_mean - unit_rows * second_mean) * inv_scale


def dot(a, b, dims):
    return lax.dot_general(a, b, ((dims[:1], dims[1:]), ((), ())), preferred_element_type=F32)


class Net:
    def __init__(self, send_sem, recv_sem):
        self.send_sem, self.recv_sem, self.copies = send_sem, recv_sem, []

    def make(self, src, dst, dev):
        i = len(self.copies)
        copy = pltpu.make_async_remote_copy(
            src_ref=src, dst_ref=dst, send_sem=self.send_sem.at[i], recv_sem=self.recv_sem.at[i],
            device_id=dev, device_id_type=MESH,
        )
        self.copies.append(copy)
        return copy

    def send(self, src, dst, dev):
        copy = self.make(src, dst, dev)
        copy.start()
        return copy


def kernel(
    n_section, state_ref, grad_ref, top_ref, loss_ref, gain_ref, wqkv_ref, wout_ref,
    rebuilt_ref, grads_ref,
    g1, g2, nb, e_buf, gc0, gc1, wq, wo, p1, q1, p2, q2, rx1, rp1, rm1, rx2, rp2, rm2,
    qkv, units, scales, probs, mixed, mgrad, dgrad, gain, out0, out1,
    send_sem, recv_sem, load_sem, out_sem,
):
    D = g1.shape[-1]
    tiles = D // 128
    na = -(-tiles * 5 // 18)
    a_w, half = na * 128, D // 2
    A0, B0, B1, A1 = (0, a_w), (a_w, half), (half, D - a_w), (D - a_w, D)
    BB, C0, C1, ALL = (a_w, D - a_w), (0, half), (half, D), (0, D)
    CH = (C0, C1)

    s = lax.axis_index("section")
    t = lax.axis_index("tensor")
    x, y, c = t // 8, (t // 2) % 4, t % 2
    ox = 1 - x
    yp, ym, y2 = (y + 1) % 4, (y + 3) % 4, (y + 2) % 4

    def dev(xx, yy, cc):
        return (s, xx * 8 + yy * 2 + cc)

    d_yp, d_ym, d_x, d_c = dev(x, yp, c), dev(x, ym, c), dev(ox, y, c), dev(x, y, 1 - c)
    d_prev = ((s + n_section - 1) % n_section, ox * 8 + y * 2 + c)
    d_next = ((s + 1) % n_section, ox * 8 + y * 2 + c)

    def row(yo, cc=None):
        return pl.multiple_of(((c if cc is None else cc) * 4 + yo) * R, R)

    def T(buf, xo, yo, cols, cc=None):
        return buf.at[xo, pl.ds(row(yo, cc), R), pl.ds(cols[0], cols[1] - cols[0])]

    def slot(buf, i, cols):
        return buf.at[i, :, pl.ds(cols[0], cols[1] - cols[0])]

    barrier = pltpu.get_barrier_semaphore()
    for d in (d_yp, d_ym, d_x, d_c, d_prev, d_next):
        pl.semaphore_signal(barrier, inc=1, device_id=d, device_id_type=MESH)
    pl.semaphore_wait(barrier, 6)

    net = Net(send_sem, recv_sem)

    def shift(first_src, src, k, cols, dst):
        cut = pl.ds(cols[0], cols[1] - cols[0])
        here = net.make(src.at[0, k, :, cut], dst, d_prev)
        net.copies.pop()
        last = net.make(first_src.at[k, :, cut], dst, d_prev)

        @pl.when(s == 0)
        def _():
            last.start()

        @pl.when(s != 0)
        def _():
            here.start()

        return last

    sh_c = [shift(top_ref, state_ref, 0, k, T(g1, x, y, k)) for k in CH]

    loads = [
        pltpu.make_async_copy(gain_ref, gain, load_sem.at[0]),
        pltpu.make_async_copy(wqkv_ref.at[0], wq, load_sem.at[1]),
        pltpu.make_async_copy(wout_ref.at[0], wo, load_sem.at[2]),
    ]
    for load in loads:
        load.start()

    def first_hop(buf, arrivals):
        one = []
        for k in range(2):
            arrivals[k].wait_recv()
            one.append([net.send(T(buf, ox, y, CH[k]), T(buf, ox, y, CH[k]), d) for d in (d_yp, d_ym, d_x)])
        return one

    def fwd(buf, xo, yo, cols, d):
        return net.send(T(buf, xo, yo, cols), T(buf, xo, yo, cols), d)

    def core_send(buf, xo, yo):
        return fwd(buf, xo, yo, ALL, d_c)

    def second_hop(buf, one):
        for copy in one[0]:
            copy.wait_recv()
        two = {}
        two["up"] = fwd(buf, ox, ym, C0, d_yp)
        two["xb0m"] = fwd(buf, ox, ym, B0, d_x)
        two["xb0p"] = fwd(buf, ox, yp, B0, d_x)
        two["a0u"] = fwd(buf, x, y, A0, d_yp)
        two["a0d"] = fwd(buf, x, y, A0, d_ym)
        for copy in one[1]:
            copy.wait_recv()
        two["down"] = fwd(buf, ox, yp, C1, d_ym)
        two["xb1p"] = fwd(buf, ox, yp, B1, d_x)
        two["xb1m"] = fwd(buf, ox, ym, B1, d_x)
        two["a1d"] = fwd(buf, x, y, A1, d_ym)
        two["a1u"] = fwd(buf, x, y, A1, d_yp)
        return two

    def third_hop(buf, two):
        three = {}
        two["up"].wait_recv()
        three["xb0"] = fwd(buf, ox, y2, B0, d_x)
        two["down"].wait_recv()
        three["xb1"] = fwd(buf, ox, y2, B1, d_x)
        two["a0u"].wait_recv()
        three["a0"] = fwd(buf, x, ym, A0, d_yp)
        two["a1d"].wait_recv()
        three["a1"] = fwd(buf, x, yp, A1, d_ym)
        return three

    def normalize(xo, yo, cc):
        r0 = row(yo, cc)
        rows = g1[xo, pl.ds(r0, R), :].astype(F32)
        unit_rows, _ = unit_norm(rows)
        nb[xo, pl.ds(r0, R), :] = (unit_rows * gain[...].astype(F32)).astype(BF16)

    def wait_rest(two, three):
        for k in ("xb0m", "xb1m", "xb0p", "xb1p", "a1u", "a0d"):
            two[k].wait_recv()

    one = first_hop(g1, sh_c)
    sh_g = [shift(loss_ref, grad_ref, 1, k, T(g2, x, y, k)) for k in CH]
    cs = [core_send(g1, ox, y)]
    loads[0].wait()
    normalize(ox, y, c)
    two = second_hop(g1, one)
    sh_e = shift(top_ref, state_ref, 1, ALL, e_buf)
    sh_gc = shift(loss_ref, grad_ref, 0, ALL, gc0)
    cs += [core_send(g1, ox, ym), core_send(g1, ox, yp), core_send(g1, x, y)]
    three = third_hop(g1, two)
    cs.append(core_send(g1, ox, y2))
    one_g = first_hop(g2, sh_g)
    cs_g = [core_send(g2, ox, y)]
    own_order = [(ox, y), (ox, ym), (ox, yp), (x, y), (ox, y2), (x, ym), (x, yp), (x, y2)]
    for xo, yo in own_order[1:5]:
        normalize(xo, yo, c)
    for i in range(5):
        cs[i].wait_recv()
        normalize(*own_order[i], 1 - c)
    wait_rest(two, three)
    cs.append(core_send(g1, x, ym))
    cs.append(core_send(g1, x, yp))
    for k in ("xb0", "xb1", "a0", "a1"):
        three[k].wait_recv()
    cs.append(core_send(g1, x, y2))
    for xo, yo in own_order[5:]:
        normalize(xo, yo, c)
    two_g = second_hop(g2, one_g)
    cs_g += [core_send(g2, ox, ym), core_send(g2, ox, yp), core_send(g2, x, y)]
    for i in range(5, 8):
        cs[i].wait_recv()
        normalize(*own_order[i], 1 - c)
    keep_c = pltpu.make_async_copy(T(g1, x, y, ALL), rebuilt_ref.at[0, 1], out_sem.at[0])
    keep_c.start()

    def project(i):
        @pl.loop(0, 3)
        def _(k):
            raw = dot(nb[i], wq[k], (1, 0))
            qkv[k, i, 0] = raw[:, :HD]
            qkv[k, i, 1] = raw[:, HD:]

    def forward(i):
        for h in range(2):
            q_unit, q_scale = unit_norm(qkv[0, i, h])
            k_unit, k_scale = unit_norm(qkv[1, i, h])
            units[0, i, h] = q_unit
            units[1, i, h] = k_unit
            scales[0, i, h] = q_scale
            scales[1, i, h] = k_scale
            scores = dot(q_unit.astype(BF16), k_unit.astype(BF16), (1, 1)) * HD ** (-0.5)
            exponent = jnp.exp(scores)
            prob = exponent * (1.0 / jnp.sum(exponent, axis=-1, keepdims=True))
            probs[i, h] = prob
            value = qkv[2, i, h].astype(BF16)
            mixed[i, :, h * HD:(h + 1) * HD] = dot(prob.astype(BF16), value, (1, 0)).astype(BF16)

    step = min(512, D)

    def out_project(i):
        @pl.loop(0, D // step)
        def _(n):
            cut = pl.ds(pl.multiple_of(n * step, step), step)
            p1[i, :, cut] = dot(mixed[i], wo[:, cut], (1, 0)).astype(BF16)

    def pair_send(p, q, i):
        half_rows = p.at[i, pl.ds(pl.multiple_of((1 - c) * 4 * R, R), 4 * R), :]
        return net.send(half_rows, q.at[i], d_c)

    def pair_sum(p, q, i, copy):
        copy.wait_recv()

        @pl.loop(0, 4)
        def _(b):
            r0 = row(b)
            q_rows = q[i, pl.ds(pl.multiple_of(b * R, R), R), :].astype(F32)
            p[i, pl.ds(r0, R), :] = (p[i, pl.ds(r0, R), :].astype(F32) + q_rows).astype(BF16)

    loads[1].wait()
    project(ox)
    three_g = third_hop(g2, two_g)
    cs_g.append(core_send(g2, ox, y2))
    project(x)
    wait_rest(two_g, three_g)
    cs_g.append(core_send(g2, x, ym))
    cs_g.append(core_send(g2, x, yp))
    forward(ox)
    loads[2].wait()
    out_project(ox)
    pair1 = [pair_send(p1, q1, ox)]
    for k in ("xb0", "xb1", "a0", "a1"):
        three_g[k].wait_recv()
    cs_g.append(core_send(g2, x, y2))
    forward(x)
    out_project(x)
    pair1.append(pair_send(p1, q1, x))
    sh_gc.wait_recv()
    hop_gc = net.send(gc0, gc1, d_x)
    sh_e.wait_recv()

    def add_to(p, xo, yo, recv, i, cols):
        cut = pl.ds(cols[0], cols[1] - cols[0])
        r0 = row(yo)
        mine = p[xo, pl.ds(r0, R), cut].astype(F32)
        p[xo, pl.ds(r0, R), cut] = (mine + recv[i, :, cut].astype(F32)).astype(BF16)

    class Scatter:
        def __init__(self, p, rx, rp, rm):
            self.p, self.rx, self.rp, self.rm, self.copies = p, rx, rp, rm, {}

        def out(self, name, xo, yo, cols, recv, i, d):
            self.copies[name] = net.send(T(self.p, xo, yo, cols), slot(recv, i, cols), d)

        def take(self, name, xo, yo, recv, i, cols):
            self.copies[name].wait_recv()
            add_to(self.p, xo, yo, recv, i, cols)

        def far(self):
            rx, rp, rm = self.rx, self.rp, self.rm
            self.out("x0", ox, y2, BB, rx, 0, d_x)
            self.out("p0", ox, y2, A0, rp, 0, d_ym)
            self.out("m0", ox, y2, A1, rm, 0, d_yp)
            self.out("x1", ox, yp, BB, rx, 1, d_x)
            self.out("x2", ox, ym, BB, rx, 2, d_x)
            self.out("p2l", ox, ym, A1, rp, 2, d_ym)
            self.out("m2l", ox, yp, A0, rm, 2, d_yp)
            self.out("x3b", ox, y, BB, rx, 3, d_x)

        def near(self):
            rp, rm = self.rp, self.rm
            self.out("p1", x, y2, A0, rp, 1, d_ym)
            self.out("m1", x, y2, A1, rm, 1, d_yp)
            self.out("p3l", x, ym, A1, rp, 3, d_ym)
            self.out("m3l", x, yp, A0, rm, 3, d_yp)

        def mid_far(self):
            rp, rm = self.rp, self.rm
            self.take("p0", ox, ym, rp, 0, A0)
            self.out("p2", ox, ym, A0, rp, 2, d_ym)
            self.take("m0", ox, yp, rm, 0, A1)
            self.out("m2", ox, yp, A1, rm, 2, d_yp)

        def mid_x(self):
            rx, rp, rm = self.rx, self.rp, self.rm
            self.take("x0", x, y2, rx, 0, BB)
            self.out("p1b", x, y2, B0, rp, 1, d_ym)
            self.out("m1b", x, y2, B1, rm, 1, d_yp)

        def mid_near(self):
            rp, rm = self.rp, self.rm
            self.take("p1", x, ym, rp, 1, A0)
            self.out("p3", x, ym, A0, rp, 3, d_ym)
            self.take("m1", x, yp, rm, 1, A1)
            self.out("m3", x, yp, A1, rm, 3, d_yp)

        def mid_x2(self):
            rx, rp, rm = self.rx, self.rp, self.rm
            self.take("x1", x, yp, rx, 1, BB)
            self.out("m3bl", x, yp, B0, rm, 3, d_yp)
            self.take("x2", x, ym, rx, 2, BB)
            self.out("p3bl", x, ym, B1, rp, 3, d_ym)

        def late_y(self):
            rp, rm = self.rp, self.rm
            self.take("p1b", x, ym, rp, 1, B0)
            self.out("p3b", x, ym, B0, rp, 3, d_ym)
            self.take("m1b", x, yp, rm, 1, B1)
            self.out("m3b", x, yp, B1, rm, 3, d_yp)

        def late_x(self):
            rx, rp, rm = self.rx, self.rp, self.rm
            self.take("p2l", ox, y, rp, 2, A1)
            self.take("m2", ox, y, rm, 2, A1)
            self.out("x3a1", ox, y, A1, rx, 3, d_x)
            self.take("m2l", ox, y, rm, 2, A0)
            self.take("p2", ox, y, rp, 2, A0)
            self.out("x3a0", ox, y, A0, rx, 3, d_x)

        def end(self):
            for name in ("x3b", "p3l", "m3l", "p3", "m3", "m3bl", "p3bl", "p3b", "m3b", "x3a1", "x3a0"):
                self.copies[name].wait_recv()

        def total(self):
            p, rx, rp, rm = self.p, self.rx, self.rp, self.rm
            mine = p[x, pl.ds(row(y), R), :].astype(F32) + rx[3].astype(F32)
            return mine + (rp[3].astype(F32) + rm[3].astype(F32))

    rs1 = Scatter(p1, rx1, rp1, rm1)
    pair_sum(p1, q1, ox, pair1[0])
    r_e = row(y)
    p1[ox, pl.ds(r_e, R), :] = (p1[ox, pl.ds(r_e, R), :].astype(F32) - e_buf[...].astype(F32)).astype(BF16)
    rs1.far()
    pair_sum(p1, q1, x, pair1[1])
    rs1.near()

    for i in range(8):
        cs_g[i].wait_recv()

    def mixed_back(i):
        mgrad[i] = dot(g2[i], wo[...], (1, 1)).astype(BF16)

    def backward(i):
        for h in range(2):
            cols = slice(h * HD, (h + 1) * HD)
            mg = mgrad[i, :, cols]
            value = qkv[2, i, h].astype(BF16)
            prob = probs[i, h]
            prob_grad = dot(mg, value, (1, 1))
            dgrad[2, i, :, cols] = dot(prob.astype(BF16), mg, (0, 0)).astype(BF16)
            inner = jnp.sum(prob_grad * prob, axis=-1, keepdims=True)
            score_grad = (prob * (prob_grad - inner) * HD ** (-0.5)).astype(BF16)
            q_unit, k_unit = units[0, i, h], units[1, i, h]
            q_part = dot(score_grad, k_unit.astype(BF16), (1, 0))
            k_part = dot(score_grad, q_unit.astype(BF16), (0, 0))
            dgrad[0, i, :, cols] = norm_back(q_part, q_unit, scales[0, i, h]).astype(BF16)
            dgrad[1, i, :, cols] = norm_back(k_part, k_unit, scales[1, i, h]).astype(BF16)

    def in_project(i):
        @pl.loop(0, D // step)
        def _(n):
            cut = pl.ds(pl.multiple_of(n * step, step), step)
            total = dot(dgrad[0, i], wq[0, cut, :], (1, 1))
            total += dot(dgrad[1, i], wq[1, cut, :], (1, 1))
            total += dot(dgrad[2, i], wq[2, cut, :], (1, 1))
            p2[i, :, cut] = total.astype(BF16)

    mixed_back(ox)
    rs1.mid_far()
    rs1.mid_x()
    mixed_back(x)
    rs1.mid_near()
    rs1.mid_x2()
    backward(ox)
    rs1.late_y()
    rs1.late_x()
    in_project(ox)
    pair2 = [pair_send(p2, q2, ox)]
    backward(x)
    rs2 = Scatter(p2, rx2, rp2, rm2)
    pair_sum(p2, q2, ox, pair2[0])
    rs2.far()
    in_project(x)
    pair2.append(pair_send(p2, q2, x))
    keep_g = pltpu.make_async_copy(T(g2, x, y, ALL), grads_ref.at[0, 0], out_sem.at[1])
    keep_g.start()
    rs1.end()
    out0[...] = (-rs1.total()).astype(BF16)
    keep_0 = pltpu.make_async_copy(out0, rebuilt_ref.at[0, 0], out_sem.at[2])
    keep_0.start()
    pair_sum(p2, q2, x, pair2[1])
    rs2.near()
    rs2.mid_far()
    rs2.mid_x()
    rs2.mid_near()
    rs2.mid_x2()
    rs2.late_y()
    rs2.late_x()
    hop_gc.wait_recv()
    rs2.end()
    normed_grad = rs2.total()
    unit_rows, inv_scale = unit_norm(g1[x, pl.ds(row(y), R), :].astype(F32))
    input_part = norm_back(normed_grad * gain[...].astype(F32), unit_rows, inv_scale)
    out1[...] = (gc1[...].astype(F32) + input_part).astype(BF16)
    keep_1 = pltpu.make_async_copy(out1, grads_ref.at[0, 1], out_sem.at[3])
    keep_1.start()
    for copy in net.copies:
        copy.wait_send()
    for keep in (keep_c, keep_g, keep_0, keep_1):
        keep.wait()


def on_device(n_section, handed_state, handed_grad, top_state, loss_grad, ln_gain, w_qkv, w_out):
    D = handed_state.shape[-1]
    width = w_out.shape[1]
    big = pltpu.VMEM((2, 8 * R, D), BF16)
    half = pltpu.VMEM((2, 4 * R, D), BF16)
    rows = pltpu.VMEM((R, D), BF16)
    recv = pltpu.VMEM((4, R, D), BF16)
    tok = 8 * R
    scratch = [
        big, big, big, rows, rows, rows,
        pltpu.VMEM((3, D, width), BF16), pltpu.VMEM((width, D), BF16),
        big, half, big, half, recv, recv, recv, recv, recv, recv,
        pltpu.VMEM((3, 2, 2, tok, HD), F32), pltpu.VMEM((2, 2, 2, tok, HD), F32), pltpu.VMEM((2, 2, 2, tok, 1), F32),
        pltpu.VMEM((2, 2, tok, tok), F32), pltpu.VMEM((2, tok, width), BF16), pltpu.VMEM((2, tok, width), BF16),
        pltpu.VMEM((3, 2, tok, width), BF16), pltpu.VMEM((1, D), BF16), rows, rows,
        pltpu.SemaphoreType.DMA((N_COPIES,)), pltpu.SemaphoreType.DMA((N_COPIES,)),
        pltpu.SemaphoreType.DMA((3,)), pltpu.SemaphoreType.DMA((4,)),
    ]
    out = jax.ShapeDtypeStruct((1, 2, R, D), BF16)
    return pl.pallas_call(
        functools.partial(kernel, n_section),
        out_shape=(out, out),
        in_specs=[pl.BlockSpec(memory_space=pl.ANY)] * 7,
        out_specs=[pl.BlockSpec(memory_space=pl.ANY)] * 2,
        scratch_shapes=scratch,
        compiler_params=pltpu.CompilerParams(
            collective_id=0, has_side_effects=True, vmem_limit_bytes=60 * 2**20
        ),
        name="sublayer_back",
    )(handed_state, handed_grad, top_state, loss_grad, ln_gain, w_qkv, w_out)


def solution(mesh):
    placed = (
        P("section", None, "tensor", None),
        P("section", None, "tensor", None),
        P(None, "tensor", None),
        P(None, "tensor", None),
        P("section", None),
        P("section", None, None, "tensor"),
        P("section", "tensor", None),
    )
    return jax.shard_map(
        functools.partial(on_device, mesh.shape["section"]),
        mesh=mesh,
        in_specs=placed,
        out_specs=(P("section", None, "tensor", None), P("section", None, "tensor", None)),
        check_vma=False,
    )
```

time: 302 us -> 97.4 us (0.32)
  waiting for transfers between devices: 204 us -> 0 us
  Pallas kernels: 0 us -> 91.2 us
  matrix products: 43.1 us -> 0 us
  other arithmetic: 17.6 us -> 0 us
  between operations: 14 us -> 0.64 us
  local copies, waits for them, and re-layouts: 16.4 us -> 3.74 us
  starting transfers between devices: 6.55 us -> 0 us
    reduce_scatter x2 -> x0, waiting for transfers between devices: 132 us -> none  [the longest x1 69 us: on_device(): lax.psum_scatter(jnp.dot(rows, out_weights, preferred_element_type=jnp.fl...]
    pallas_call x0 -> x1, Pallas kernels: none -> 91.2 us  [on_device(): pl.pallas_call(functools.partial(kernel, n_section), out_shape=(out, out)...]
    all_gather x2 -> x0, waiting for transfers between devices: 43 us -> none  [the longest x1 23.5 us: on_device(): lax.all_gather(normed, 'tensor', axis=0, tiled=True)]
    dot_general x12 -> x0, matrix products: 40.7 us -> none  [the longest x3 10.8 us: on_device(): jnp.einsum('tc,dc->td', rows, weights[member], preferred_element_type=jnp...]
    ppermute x2 -> x0, waiting for transfers between devices: 28.7 us -> none  [shifted(): return lax.ppermute(array, axis, pairs)]
    reduce_sum x7 -> x0, other arithmetic: 7.55 us -> none  [the longest x2 4.73 us: unit_norm(): row_mean = jnp.mean(values, axis=-1, keepdims=True)]
    another operation x4 -> x0, local copies, waits for them, and re-layouts: 6.41 us -> none  [the longest x2 4.13 us: on_device(): query_raw = projected[:, 0].reshape(images, TOK, local_heads, HD)]
    ppermute x2 -> x0, starting transfers between devices: 6.2 us -> none  [shifted(): return lax.ppermute(array, axis, pairs)]
  transfers between devices with their start and end apart: 6 -> 0, of which waited for: 6 -> 0; matrix products, arithmetic and copies ran while one was open for 11% -> 0% of each run, Pallas kernels for 0% -> 0%
where the time goes in v1:
time: 97.4 us; the launch traced here: 95.6 us
  Pallas kernels  91.2 us (94%)
  local copies, waits for them, and re-layouts  3.74 us (4%)
    pallas_call x1, Pallas kernels, on_device(): pl.pallas_call(functools.partial(kernel, n_section), out_shape=(out, out)...  91.2 us
    unnamed x2, local copies, waits for them, and re-layouts  3.74 us

profile of v1, /device:TPU:4, one launch (start us, length us, event | category | flops | bytes accessed | tf_op | source)
XLA Modules:
  0.0 95.6 jit_solution(1021060608173582135)
XLA Ops:
  0.6 91.2 %sublayer_back.1 = (bf16[1,2,32,4096]{3,2,1,0:T(8,128)(2,1)}, bf16[1,2,32,4096]{3,2,1,0:T(8,128)(2,1)}) custom-call(bf16[1,2,32,4096]{3,2,1,0:T(8,128)(2,1)} %state_ref.1, bf16[1,2,32,4096]{3,2,1,0:T(8,128)(2,1)} %grad_ref.1, bf16[2,32,4096]{2,1,0:T(8,128)(2,1)} %top_ref.1, bf16[2,32,4096]{2,1,0:T(8,128)(2,1)} %loss_ref.1, bf16[1,4096]{1,0:T(2,128)(2,1)} %gain_ref.1, ...), custom_call_target="tpu_custom_call" | custom-call | tf_op jit(solution)/shard_map/sublayer_back/pallas_call | solution.py:470
  91.9 1.9 %copy.11 = bf16[1,2,32,4096]{3,2,1,0:T(8,128)(2,1)} copy(bf16[1,2,32,4096]{3,2,1,0:T(8,128)(2,1)} %get-tuple-element.4) | data formatting | bytes 1048576
  93.7 1.9 %copy.12 = bf16[1,2,32,4096]{3,2,1,0:T(8,128)(2,1)} copy(bf16[1,2,32,4096]{3,2,1,0:T(8,128)(2,1)} %get-tuple-element.5) | data formatting | bytes 1048576

commit v2 on v0

v2 whole, which is shorter than its diff:
```python
import functools

import jax
import jax.numpy as jnp
from jax import lax
from jax.experimental import pallas as pl
from jax.experimental.pallas import tpu as pltpu
from jax.sharding import PartitionSpec as P

HD = 128
MESH = pl.DeviceIdType.MESH
F32 = jnp.float32
BF16 = jnp.bfloat16
R = 32
N_SHIFT, N_SEND, N_RECV = 10, 40, 93
ORDER = (
    0, 1, 2, 3, 4, 5, 6, 7, 8, 12, 17, 16, 20, 21, 10, 11, 28, 72, 9, 14, 23, 73, 37, 24, 13, 38, 36, 40, 30, 76,
    15, 32, 80, 41, 164, 18, 64, 77, 19, 25, 29, 74, 81, 26, 44, 43, 75, 22, 39, 46, 47, 42, 31, 78, 33, 82, 45, 53,
    57, 79, 34, 88, 27, 48, 56, 60, 89, 49, 51, 59, 66, 68, 92, 50, 52, 65, 83, 117, 84, 54, 55, 85, 94, 96, 98,
    100, 35, 116, 86, 123, 122, 87, 102, 58, 61, 62, 67, 124, 125, 103, 63, 69, 70, 118, 106, 130, 131, 90, 120,
    108, 91, 110, 112, 114, 119, 126, 127, 93, 71, 121, 134, 128, 129, 95, 97, 148, 145, 99, 101, 139, 104, 132,
    133, 105, 140, 107, 136, 135, 137, 138, 109, 111, 141, 146, 147, 143, 113, 115, 150, 153, 142, 152, 149, 165,
    144, 157, 154, 151, 163, 156, 159, 155, 158, 161, 160, 162, 166,
)


def mean_last(values):
    return jnp.mean(values, axis=-1, keepdims=True)


def unit_norm(values):
    centred = values - mean_last(values)
    inv_scale = lax.rsqrt(mean_last(centred * centred) + 1e-06)
    return centred * inv_scale, inv_scale


def norm_back(grad_unit, unit_rows, inv_scale):
    first_mean = mean_last(grad_unit)
    second_mean = mean_last(grad_unit * unit_rows)
    return (grad_unit - first_mean - unit_rows * second_mean) * inv_scale


def dot(a, b, dims):
    return lax.dot_general(a, b, ((dims[:1], dims[1:]), ((), ())), preferred_element_type=F32)


class Copy:
    def __init__(self, src, dst, send_sem, recv_sem, dev):
        self.src, self.dst, self.send_sem, self.recv_sem, self.dev = src, dst, send_sem, recv_sem, dev

    def make(self):
        return pltpu.make_async_remote_copy(
            src_ref=self.src(), dst_ref=self.dst(), send_sem=self.send_sem, recv_sem=self.recv_sem,
            device_id=self.dev, device_id_type=MESH,
        )

    def start(self):
        self.make().start()

    def wait_recv(self):
        self.make().wait_recv()

    def wait_send(self):
        self.make().wait_send()


class Net:
    def __init__(self, send_sem, recv_sem):
        self.send_sem, self.recv_sem, self.sent, self.at, self.used = send_sem, recv_sem, [], {}, 0

    def recv(self, key, count=1):
        if key not in self.at:
            self.at[key], self.used = self.used, self.used + count
        return self.at[key]

    def copy(self, src, dst, dev, key):
        k = len(self.sent)
        if k >= N_SEND:
            self.sent[k - N_SEND].wait_send()
        made = Copy(src, dst, self.send_sem.at[N_SHIFT + k % N_SEND], self.recv_sem.at[self.recv(key)], dev)
        self.sent.append(made)
        return made

    def send(self, src, dst, dev, key):
        made = self.copy(src, dst, dev, key)
        made.start()
        return made


def kernel(
    n_section, state_ref, grad_ref, top_ref, loss_ref, gain_ref, wqkv_ref, wout_ref,
    first_ref, kept_c_ref, kept_g_ref, second_ref,
    g1, g2, nb, e_buf, gc0, gc1, wq, wo, p1, q1, p2, q2, rx1, rp1, rm1, rx2, rp2, rm2,
    qkv, units, scales, probs, mixed, mgrad, dgrad, gain, out0, out1, own_unit, own_scale,
    send_sem, recv_sem, pair_sem, load_sem, out_sem,
):
    D = g1.shape[-1]
    half, width = D // 2, wo.shape[0]
    a_w = -(-D // 128 * 5 // 16) * 128
    A0, B0, B1, A1 = (0, a_w), (a_w, half), (half, D - a_w), (D - a_w, D)
    BB, ALL = (a_w, D - a_w), (0, D)
    CH = (A0, B0, B1, A1)

    s = lax.axis_index("section")
    t = lax.axis_index("tensor")
    x, y, c = t // 8, (t // 2) % 4, t % 2
    ox = 1 - x
    yp, ym, y2 = (y + 1) % 4, (y + 3) % 4, (y + 2) % 4

    def dev(xx, yy, cc):
        return (s, xx * 8 + yy * 2 + cc)

    d_yp, d_ym, d_x, d_c = dev(x, yp, c), dev(x, ym, c), dev(ox, y, c), dev(x, y, 1 - c)
    d_prev = ((s + n_section - 1) % n_section, ox * 8 + y * 2 + c)
    d_next = ((s + 1) % n_section, ox * 8 + y * 2 + c)

    def row(yo, cc=None):
        return pl.multiple_of(((c if cc is None else cc) * 4 + yo) * R, R)

    def T(buf, xo, yo, cols, cc=None):
        return buf.at[xo, pl.ds(row(yo, cc), R), pl.ds(cols[0], cols[1] - cols[0])]

    def slot(buf, i, cols):
        return buf.at[i, :, pl.ds(cols[0], cols[1] - cols[0])]

    barrier = pltpu.get_barrier_semaphore()
    for d in (d_yp, d_ym, d_x, d_c, d_prev, d_next):
        pl.semaphore_signal(barrier, inc=1, device_id=d, device_id_type=MESH)
    pl.semaphore_wait(barrier, 6)

    net = Net(send_sem, recv_sem)
    copies, tasks = {}, {}
    shared = {}
    for p in "12":
        shared |= {p + m: p + "g5" for m in ("a3u", "b1m", "b2m")}
        shared |= {p + m: p + "g6" for m in ("a0d", "b1p", "b2p")}
        shared |= {p + m: p + "g7" for m in ("a0", "a3", "b1", "b2")}
    for r in ("r1", "r2"):
        shared |= {r + m: r + "gx" for m in ("x3b", "x3a3", "x3a0")}
        shared |= {r + m: r + "gp" for m in ("p3l", "p3", "p3bl", "p3b")}
        shared |= {r + m: r + "gm" for m in ("m3l", "m3", "m3bl", "m3b")}
    once = ["x0", "x1", "x2", "p0", "m0", "p2l", "m2l", "p1", "m1", "p2", "m2", "p1b", "m1b", "gx", "gp", "gm"]
    again = {"r2" + m: f"1{d}{k}" for m, (d, k) in zip(once, [(d, k) for d in "huds" for k in range(4)])}

    def recv_key(name):
        name = shared.get(name, name)
        return again.get(name, name)

    shifts = []

    def shift(name, first_src, src, k, cols, dst):
        cut = pl.ds(cols[0], cols[1] - cols[0])
        sems = send_sem.at[len(shifts)], recv_sem.at[net.recv(name)]
        last = Copy(lambda: first_src.at[k, :, cut], dst, *sems, d_prev)
        shifts.append(last)
        here = Copy(lambda: src.at[0, k, :, cut], dst, *sems, d_prev)
        copies[name] = last

        @pl.when(s == 0)
        def _():
            last.start()

        @pl.when(s != 0)
        def _():
            here.start()

    for k in range(4):
        shift(f"1h{k}", top_ref, state_ref, 0, CH[k], functools.partial(T, g1, x, y, CH[k]))
    for k in range(4):
        shift(f"2h{k}", loss_ref, grad_ref, 1, CH[k], functools.partial(T, g2, x, y, CH[k]))
    shift("e", top_ref, state_ref, 1, ALL, lambda: e_buf)
    shift("gc", loss_ref, grad_ref, 0, ALL, lambda: gc0)

    def together(key, region):
        copies[key] = Copy(region, region, net.send_sem.at[0], net.recv_sem.at[net.recv(recv_key(key))], d_c)

    loads = [
        pltpu.make_async_copy(gain_ref, gain, load_sem.at[0]),
        pltpu.make_async_copy(wout_ref.at[0], wo, load_sem.at[1]),
    ] + [
        pltpu.make_async_copy(wqkv_ref.at[0, k], wq.at[:, pl.ds(k * width, width)], load_sem.at[2 + k]) for k in range(3)
    ]
    for load in loads:
        load.start()

    places = ((ox, y), (ox, ym), (ox, yp), (ox, y2), (x, y), (x, ym), (x, yp), (x, y2))
    slots = (
        ("h0", "h1", "h2", "h3"), ("u0", "u1", "u2", "u3"), ("d0", "d1", "d2", "d3"), ("f0", "f1", "f2", "f3"),
        ("s0", "s1", "s2", "s3"), ("a0u", "g5"), ("a3d", "g6"), ("g7",),
    )
    images = {"o": ox, "x": x}
    loaded = set()

    def need(i):
        if i not in loaded:
            loaded.add(i)
            loads[i].wait()

    def task(name, arrivals, run):
        tasks[name] = (tuple(arrivals), run)

    def sending(name, arrivals, src, dst, d):
        def run():
            copies[name] = net.send(src, dst, d, recv_key(name))

        task(name, arrivals, run)

    def forwarding(name, arrivals, buf, xo, yo, cols, d):
        sending(name, arrivals, lambda: T(buf, xo, yo, cols), lambda: T(buf, xo, yo, cols), d)

    for p, buf in (("1", g1), ("2", g2)):
        for k in range(4):
            forwarding(f"{p}u{k}", (f"{p}h{k}",), buf, ox, y, CH[k], d_yp)
            forwarding(f"{p}d{k}", (f"{p}h{k}",), buf, ox, y, CH[k], d_ym)
            forwarding(f"{p}s{k}", (f"{p}h{k}",), buf, ox, y, CH[k], d_x)
        for k in (0, 1):
            forwarding(f"{p}f{k}", (f"{p}u{k}",), buf, ox, ym, CH[k], d_yp)
        for k in (2, 3):
            forwarding(f"{p}f{k}", (f"{p}d{k}",), buf, ox, yp, CH[k], d_ym)
        for k in (0, 3):
            forwarding(f"{p}a{k}u", (f"{p}s{k}",), buf, x, y, CH[k], d_yp)
            forwarding(f"{p}a{k}d", (f"{p}s{k}",), buf, x, y, CH[k], d_ym)
        for k in (1, 2):
            forwarding(f"{p}b{k}m", (f"{p}u{k}",), buf, ox, ym, CH[k], d_x)
            forwarding(f"{p}b{k}p", (f"{p}d{k}",), buf, ox, yp, CH[k], d_x)
            forwarding(f"{p}b{k}", (f"{p}f{k}",), buf, ox, y2, CH[k], d_x)
        together(f"{p}g5", functools.partial(T, buf, x, ym, (a_w, D)))
        together(f"{p}g6", functools.partial(T, buf, x, yp, (0, D - a_w)))
        together(f"{p}g7", functools.partial(T, buf, x, y2, ALL))
        forwarding(f"{p}a0", (f"{p}a0u",), buf, x, ym, CH[0], d_yp)
        forwarding(f"{p}a3", (f"{p}a3d",), buf, x, yp, CH[3], d_ym)
        for j in range(8):
            forwarding(f"{p}c{j}", [p + m for m in slots[j]], buf, *places[j], ALL, d_c)

    def normalize(place, cc):
        need(0)
        xo, yo = place

        part = pl.ds(row(yo, cc), R)
        unit_rows, _ = unit_norm(g1[xo, part, :].astype(F32))
        nb[xo, part, :] = (unit_rows * gain[...].astype(F32)).astype(BF16)

    for j in range(8):
        task(f"no{j}", ["1" + m for m in slots[j]], functools.partial(normalize, places[j], c))
        task(f"nx{j}", (f"1c{j}",), functools.partial(normalize, places[j], 1 - c))

    def project(i):
        for k in range(3):
            need(2 + k)

        @pl.loop(0, 3)
        def _(k):
            raw = dot(nb[i], wq[:, pl.ds(pl.multiple_of(k * width, width), width)], (1, 0))
            qkv[k, i, 0] = raw[:, :HD]
            qkv[k, i, 1] = raw[:, HD:]

    def head(h, base=0):
        return slice(base + h * HD, base + (h + 1) * HD)

    def forward(i):
        for h in range(2):
            q_unit, q_scale = unit_norm(qkv[0, i, h])
            k_unit, k_scale = unit_norm(qkv[1, i, h])
            units[0, i, h] = q_unit
            units[1, i, h] = k_unit
            scales[0, i, h] = q_scale
            scales[1, i, h] = k_scale
            scores = dot(q_unit.astype(BF16), k_unit.astype(BF16), (1, 1)) * HD ** (-0.5)
            exponent = jnp.exp(scores)
            prob = exponent * (1.0 / jnp.sum(exponent, axis=-1, keepdims=True))
            probs[i, h] = prob
            value = qkv[2, i, h].astype(BF16)
            mixed[i, :, head(h)] = dot(prob.astype(BF16), value, (1, 0)).astype(BF16)

    mine0 = pl.multiple_of(c * 4 * R, R)
    other0 = pl.multiple_of((1 - c) * 4 * R, R)
    step = D // 4

    pair_sent = []

    def in_steps(names, p, q, i, value):
        at = net.recv(names[0] + names[2:], 4)
        for copy in pair_sent:
            copy.wait_send()
        pair_sent.clear()

        def pair_copy(n):
            cut = pl.ds(n * step if isinstance(n, int) else pl.multiple_of(n * step, step), step)
            src = functools.partial(lambda cut: p.at[i, pl.ds(other0, 4 * R), cut], cut)
            dst = functools.partial(lambda cut: q.at[i, :, cut], cut)
            return Copy(src, dst, pair_sem.at[n], recv_sem.at[at + n], d_c)

        @pl.loop(0, 4)
        def _(n):
            cut = pl.ds(pl.multiple_of(n * step, step), step)
            p[i, :, cut] = value(cut).astype(BF16)
            pair_copy(n).start()

        for n in range(4):
            copies[f"{names}{n}"] = pair_copy(n)
            pair_sent.append(copies[f"{names}{n}"])

    def out_project(names, i):
        need(1)
        in_steps(names, p1, q1, i, lambda cut: dot(mixed[i], wo[:, cut], (1, 0)))

    def in_project(names, i):
        in_steps(names, p2, q2, i, lambda cut: dot(dgrad[i], wq[cut, :], (1, 1)))

    def pair_sum(p, q, i, n):
        @pl.loop(0, 4)
        def _(b):
            cut = pl.ds(n * step, step)
            mine = pl.ds(pl.multiple_of(mine0 + b * R, R), R)
            total = p[i, mine, cut].astype(F32) + q[i, pl.ds(pl.multiple_of(b * R, R), R), cut].astype(F32)
            p[i, mine, cut] = total.astype(BF16)

    def mixed_back(i):
        mgrad[i] = dot(g2[i], wo[...], (1, 1)).astype(BF16)

    def backward(i):
        for h in range(2):
            mg = mgrad[i, :, head(h)]
            value = qkv[2, i, h].astype(BF16)
            prob = probs[i, h]
            prob_grad = dot(mg, value, (1, 1))
            v_grad = dot(prob.astype(BF16), mg, (0, 0)).astype(BF16)
            inner = jnp.sum(prob_grad * prob, axis=-1, keepdims=True)
            score_grad = (prob * (prob_grad - inner) * HD ** (-0.5)).astype(BF16)
            q_unit, k_unit = units[0, i, h], units[1, i, h]
            q_part = dot(score_grad, k_unit.astype(BF16), (1, 0))
            k_part = dot(score_grad, q_unit.astype(BF16), (0, 0))
            dgrad[i, :, head(h)] = norm_back(q_part, q_unit, scales[0, i, h]).astype(BF16)
            dgrad[i, :, head(h, width)] = norm_back(k_part, k_unit, scales[1, i, h]).astype(BF16)
            dgrad[i, :, head(h, 2 * width)] = v_grad

    for im, i in images.items():
        places_of = range(0, 4) if im == "o" else range(4, 8)
        task(f"pj{im}", (), functools.partial(project, i))
        task(f"fw{im}", (), functools.partial(forward, i))
        arrivals = [f"2c{j}" for j in places_of] + ["2" + m for j in places_of for m in slots[j]]
        task(f"mb{im}", arrivals, functools.partial(mixed_back, i))
        task(f"bw{im}", (), functools.partial(backward, i))
        task(f"op{im}", (), functools.partial(out_project, f"q1{im}", i))
        task(f"ip{im}", (), functools.partial(in_project, f"q2{im}", i))
        for n in range(4):
            task(f"ps1{im}{n}", (f"q1{im}{n}",), functools.partial(pair_sum, p1, q1, i, n))
            task(f"ps2{im}{n}", (f"q2{im}{n}",), functools.partial(pair_sum, p2, q2, i, n))

    def subtract():
        r0 = row(y)
        p1[ox, pl.ds(r0, R), :] = (p1[ox, pl.ds(r0, R), :].astype(F32) - e_buf[...].astype(F32)).astype(BF16)

    task("es", ("e",), subtract)
    sending("hop", ("gc",), lambda: gc0, lambda: gc1, d_x)

    def add_to(p, xo, yo, recv, i, cols):
        cut = pl.ds(cols[0], cols[1] - cols[0])
        r0 = row(yo)
        mine = p[xo, pl.ds(r0, R), cut].astype(F32)
        p[xo, pl.ds(r0, R), cut] = (mine + recv[i, :, cut].astype(F32)).astype(BF16)

    def scatter(n, p, rx, rp, rm):
        def step(name, adds, sends):
            def run():
                for xo, yo, recv, i, cols, _ in adds:
                    add_to(p, xo, yo, recv, i, cols)
                for copy, xo, yo, cols, recv, i, d in sends:
                    src = functools.partial(T, p, xo, yo, cols)
                    copies[n + copy] = net.send(src, functools.partial(slot, recv, i, cols), d, recv_key(n + copy))

            task(n + name, [n + add[-1] for add in adds], run)

        step("x0", (), (("x0", ox, y2, BB, rx, 0, d_x),))
        step("x1", (), (("x1", ox, yp, BB, rx, 1, d_x),))
        step("x2", (), (("x2", ox, ym, BB, rx, 2, d_x),))
        step("x3b", (), (("x3b", ox, y, BB, rx, 3, d_x),))
        step("p0", (), (("p0", ox, y2, A0, rp, 0, d_ym),))
        step("m0", (), (("m0", ox, y2, A1, rm, 0, d_yp),))
        step("p2l", (), (("p2l", ox, ym, A1, rp, 2, d_ym),))
        step("m2l", (), (("m2l", ox, yp, A0, rm, 2, d_yp),))
        step("p1", (), (("p1", x, y2, A0, rp, 1, d_ym),))
        step("m1", (), (("m1", x, y2, A1, rm, 1, d_yp),))
        step("p3l", (), (("p3l", x, ym, A1, rp, 3, d_ym),))
        step("m3l", (), (("m3l", x, yp, A0, rm, 3, d_yp),))
        step("p2", ((ox, ym, rp, 0, A0, "p0"),), (("p2", ox, ym, A0, rp, 2, d_ym),))
        step("m2", ((ox, yp, rm, 0, A1, "m0"),), (("m2", ox, yp, A1, rm, 2, d_yp),))
        step("p3", ((x, ym, rp, 1, A0, "p1"),), (("p3", x, ym, A0, rp, 3, d_ym),))
        step("m3", ((x, yp, rm, 1, A1, "m1"),), (("m3", x, yp, A1, rm, 3, d_yp),))
        step("tx0", ((x, y2, rx, 0, BB, "x0"),), (("p1b", x, y2, B0, rp, 1, d_ym), ("m1b", x, y2, B1, rm, 1, d_yp)))
        step("tx1", ((x, yp, rx, 1, BB, "x1"),), (("m3bl", x, yp, B0, rm, 3, d_yp),))
        step("tx2", ((x, ym, rx, 2, BB, "x2"),), (("p3bl", x, ym, B1, rp, 3, d_ym),))
        step("p3b", ((x, ym, rp, 1, B0, "p1b"),), (("p3b", x, ym, B0, rp, 3, d_ym),))
        step("m3b", ((x, yp, rm, 1, B1, "m1b"),), (("m3b", x, yp, B1, rm, 3, d_yp),))
        step("x3a3", ((ox, y, rp, 2, A1, "p2l"), (ox, y, rm, 2, A1, "m2")), (("x3a3", ox, y, A1, rx, 3, d_x),))
        step("x3a0", ((ox, y, rm, 2, A0, "m2l"), (ox, y, rp, 2, A0, "p2")), (("x3a0", ox, y, A0, rx, 3, d_x),))

    ends = ("gx", "gp", "gm")
    for r, buffers in (("r1", (rx1, rp1, rm1)), ("r2", (rx2, rp2, rm2))):
        for m, recv in zip(ends, buffers):
            together(r + m, functools.partial(slot, recv, 3, ALL))
    scatter("r1", p1, rx1, rp1, rm1)
    scatter("r2", p2, rx2, rp2, rm2)

    def total(p, rx, rp, rm):
        mine = p[x, pl.ds(row(y), R), :].astype(F32) + rx[3].astype(F32)
        return mine + (rp[3].astype(F32) + rm[3].astype(F32))

    keeps = [
        pltpu.make_async_copy(T(g1, x, y, ALL), kept_c_ref, out_sem.at[0]),
        pltpu.make_async_copy(T(g2, x, y, ALL), kept_g_ref, out_sem.at[1]),
        pltpu.make_async_copy(out0, first_ref, out_sem.at[2]),
        pltpu.make_async_copy(out1, second_ref, out_sem.at[3]),
    ]

    def finish_first():
        keeps[0].start()
        keeps[1].start()
        out0[...] = (-total(p1, rx1, rp1, rm1)).astype(BF16)
        keeps[2].start()

    def prepare():
        unit_rows, inv_scale = unit_norm(g1[x, pl.ds(row(y), R), :].astype(F32))
        own_unit[...] = unit_rows
        own_scale[...] = inv_scale

    def finish_second():
        normed_grad = total(p2, rx2, rp2, rm2)
        input_part = norm_back(normed_grad * gain[...].astype(F32), own_unit[...], own_scale[...])
        out1[...] = (gc1[...].astype(F32) + input_part).astype(BF16)
        keeps[3].start()

    task("prep", (), prepare)

    task("fin1", ["r1" + m for m in ends], finish_first)
    task("fin2", ["r2" + m for m in ends] + ["hop"], finish_second)

    arrived = set()
    names = list(tasks)
    for number in ORDER:
        arrivals, run = tasks.pop(names[number])
        for copy in arrivals:
            if copy not in arrived:
                arrived.add(copy)
                copies[copy].wait_recv()
        run()
    assert not tasks and arrived == set(copies) - set(shared)
    for copy in shifts + net.sent[-N_SEND:] + pair_sent:
        copy.wait_send()
    for keep in keeps:
        keep.wait()


def on_device(n_section, handed_state, handed_grad, top_state, loss_grad, ln_gain, w_qkv, w_out):
    D = handed_state.shape[-1]
    width = w_out.shape[1]
    big = pltpu.VMEM((2, 8 * R, D), BF16)
    half = pltpu.VMEM((2, 4 * R, D), BF16)
    rows = pltpu.VMEM((R, D), BF16)
    recv = pltpu.VMEM((4, R, D), BF16)
    tok = 8 * R
    scratch = [
        big, big, big, rows, rows, rows,
        pltpu.VMEM((D, 3 * width), BF16), pltpu.VMEM((width, D), BF16),
        big, half, big, half, recv, recv, recv, recv, recv, recv,
        pltpu.VMEM((3, 2, 2, tok, HD), F32), pltpu.VMEM((2, 2, 2, tok, HD), F32), pltpu.VMEM((2, 2, 2, tok, 1), F32),
        pltpu.VMEM((2, 2, tok, tok), F32), pltpu.VMEM((2, tok, width), BF16), pltpu.VMEM((2, tok, width), BF16),
        pltpu.VMEM((2, tok, 3 * width), BF16), pltpu.VMEM((1, D), BF16), rows, rows, pltpu.VMEM((R, D), F32), pltpu.VMEM((R, 1), F32),
        pltpu.SemaphoreType.DMA((N_SHIFT + N_SEND,)), pltpu.SemaphoreType.DMA((N_RECV,)), pltpu.SemaphoreType.DMA((4,)),
        pltpu.SemaphoreType.DMA((5,)), pltpu.SemaphoreType.DMA((4,)),
    ]
    block = jax.ShapeDtypeStruct((R, D), BF16)
    out = jax.ShapeDtypeStruct((1, 2, R, D), BF16)
    anywhere = pl.BlockSpec(memory_space=pl.ANY)
    blocks = pl.pallas_call(
        functools.partial(kernel, n_section),
        out_shape=(block,) * 4,
        in_specs=[anywhere] * 7,
        out_specs=[anywhere] * 4,
        scratch_shapes=scratch,
        compiler_params=pltpu.CompilerParams(
            collective_id=0, has_side_effects=True, vmem_limit_bytes=60 * 2**20
        ),
        name="sublayer_back",
    )(handed_state, handed_grad, top_state, loss_grad, ln_gain, w_qkv, w_out)
    vmem = pl.BlockSpec(memory_space=pltpu.VMEM)
    return pl.pallas_call(
        assemble,
        out_shape=(out, out),
        in_specs=[anywhere] * 4,
        out_specs=[anywhere] * 2,
        scratch_shapes=[pltpu.VMEM((4, R, D), BF16), pltpu.SemaphoreType.DMA((4,)), pltpu.SemaphoreType.DMA((4,))],
        name="assemble",
    )(*blocks)


def assemble(first_ref, kept_c_ref, kept_g_ref, second_ref, rebuilt_ref, grads_ref, rows, in_sem, out_sem):
    ins = (first_ref, kept_c_ref, kept_g_ref, second_ref)
    outs = (rebuilt_ref.at[0, 0], rebuilt_ref.at[0, 1], grads_ref.at[0, 0], grads_ref.at[0, 1])
    loads = [pltpu.make_async_copy(src, rows.at[i], in_sem.at[i]) for i, src in enumerate(ins)]
    stores = [pltpu.make_async_copy(rows.at[i], dst, out_sem.at[i]) for i, dst in enumerate(outs)]
    for load in loads:
        load.start()
    for load, store in zip(loads, stores):
        load.wait()
        store.start()
    for store in stores:
        store.wait()


def solution(mesh):
    placed = (
        P("section", None, "tensor", None),
        P("section", None, "tensor", None),
        P(None, "tensor", None),
        P(None, "tensor", None),
        P("section", None),
        P("section", None, None, "tensor"),
        P("section", "tensor", None),
    )
    return jax.shard_map(
        functools.partial(on_device, mesh.shape["section"]),
        mesh=mesh,
        in_specs=placed,
        out_specs=(P("section", None, "tensor", None), P("section", None, "tensor", None)),
        check_vma=False,
    )
```

time: 302 us -> 74.3 us (0.25)
  waiting for transfers between devices: 204 us -> 0 us
  Pallas kernels: 0 us -> 72.1 us
  matrix products: 43.1 us -> 0 us
  other arithmetic: 17.6 us -> 0 us
  local copies, waits for them, and re-layouts: 16.4 us -> 0 us
  between operations: 14 us -> 0.8 us
  starting transfers between devices: 6.55 us -> 0 us
    reduce_scatter x2 -> x0, waiting for transfers between devices: 132 us -> none  [the longest x1 69 us: on_device(): lax.psum_scatter(jnp.dot(rows, out_weights, preferred_element_type=jnp.fl...]
    pallas_call x0 -> x2, Pallas kernels: none -> 72.1 us  [the longest x1 70.1 us: on_device(): pl.pallas_call(functools.partial(kernel, n_section), out_shape=(block,) *...]
    all_gather x2 -> x0, waiting for transfers between devices: 43 us -> none  [the longest x1 23.5 us: on_device(): lax.all_gather(normed, 'tensor', axis=0, tiled=True)]
    dot_general x12 -> x0, matrix products: 40.7 us -> none  [the longest x3 10.8 us: on_device(): jnp.einsum('tc,dc->td', rows, weights[member], preferred_element_type=jnp...]
    ppermute x2 -> x0, waiting for transfers between devices: 28.7 us -> none  [shifted(): return lax.ppermute(array, axis, pairs)]
    reduce_sum x7 -> x0, other arithmetic: 7.55 us -> none  [the longest x2 4.73 us: unit_norm(): row_mean = jnp.mean(values, axis=-1, keepdims=True)]
    another operation x4 -> x0, local copies, waits for them, and re-layouts: 6.41 us -> none  [the longest x2 4.13 us: on_device(): query_raw = projected[:, 0].reshape(images, TOK, local_heads, HD)]
    ppermute x2 -> x0, starting transfers between devices: 6.2 us -> none  [shifted(): return lax.ppermute(array, axis, pairs)]
  transfers between devices with their start and end apart: 6 -> 0, of which waited for: 6 -> 0; matrix products, arithmetic and copies ran while one was open for 11% -> 0% of each run, Pallas kernels for 0% -> 0%
where the time goes in v2:
time: 74.3 us; the launch traced here: 72.9 us
  Pallas kernels  72.1 us (97%)
  between operations  0.8 us (1%)
    pallas_call x1, Pallas kernels, on_device(): pl.pallas_call(functools.partial(kernel, n_section), out_shape=(block,) *...  70.1 us
    pallas_call x1, Pallas kernels, on_device(): pl.pallas_call(assemble, out_shape=(out, out), in_specs=[anywhere] * 4, o...  1.98 us

profile of v2, /device:TPU:4, one launch (start us, length us, event | category | flops | bytes accessed | tf_op | source)
XLA Modules:
  0.0 72.9 jit_solution(15960605095453498348)
XLA Ops:
  0.6 70.1 %sublayer_back.1 = (bf16[32,4096]{1,0:T(8,128)(2,1)}, bf16[32,4096]{1,0:T(8,128)(2,1)}, bf16[32,4096]{1,0:T(8,128)(2,1)}, bf16[32,4096]{1,0:T(8,128)(2,1)}) custom-call(bf16[1,2,32,4096]{3,2,1,0:T(8,128)(2,1)} %state_ref.1, bf16[1,2,32,4096]{3,2,1,0:T(8,128)(2,1)} %grad_ref.1, bf16[2,32,4096]{2,1,0:T(8,128)(2,1)} %top_ref.1, bf16[2,32,4096]{2,1,0:T(8,128)(2,1)} %loss_ref.1, ...), custom_call_target="tpu_custom_call" | custom-call | tf_op jit(solution)/shard_map/sublayer_back/pallas_call | solution.py:475
  70.7 2.0 %assemble.1 = (bf16[1,2,32,4096]{3,2,1,0:T(8,128)(2,1)}, bf16[1,2,32,4096]{3,2,1,0:T(8,128)(2,1)}) custom-call(bf16[32,4096]{1,0:T(8,128)(2,1)} %get-tuple-element.6.first_ref, bf16[32,4096]{1,0:T(8,128)(2,1)} %get-tuple-element.7.kept_c_ref, bf16[32,4096]{1,0:T(8,128)(2,1)} %get-tuple-element.8.kept_g_ref, bf16[32,4096]{1,0:T(8,128)(2,1)} %get-tuple-element.9.second_ref), custom_call_target="tpu_custom_call" | custom-call | tf_op jit(solution)/shard_map/assemble/pallas_call | solution.py:487

commit v3 on v2

--- a/solution.py
+++ b/solution.py
@@ -91,7 +91,7 @@
     n_section, state_ref, grad_ref, top_ref, loss_ref, gain_ref, wqkv_ref, wout_ref,
     first_ref, kept_c_ref, kept_g_ref, second_ref,
     g1, g2, nb, e_buf, gc0, gc1, wq, wo, p1, q1, p2, q2, rx1, rp1, rm1, rx2, rp2, rm2,
-    qkv, units, scales, probs, mixed, mgrad, dgrad, gain, out0, out1, own_unit, own_scale,
+    qkv, units, scales, probs, mixed, mgrad, dgrad, gain, own_unit, own_scale,
     send_sem, recv_sem, pair_sem, load_sem, out_sem,
 ):
     D = g1.shape[-1]
@@ -409,15 +409,12 @@
     keeps = [
         pltpu.make_async_copy(T(g1, x, y, ALL), kept_c_ref, out_sem.at[0]),
         pltpu.make_async_copy(T(g2, x, y, ALL), kept_g_ref, out_sem.at[1]),
-        pltpu.make_async_copy(out0, first_ref, out_sem.at[2]),
-        pltpu.make_async_copy(out1, second_ref, out_sem.at[3]),
     ]
 
     def finish_first():
         keeps[0].start()
         keeps[1].start()
-        out0[...] = (-total(p1, rx1, rp1, rm1)).astype(BF16)
-        keeps[2].start()
+        first_ref[...] = (-total(p1, rx1, rp1, rm1)).astype(BF16)
 
     def prepare():
         unit_rows, inv_scale = unit_norm(g1[x, pl.ds(row(y), R), :].astype(F32))
@@ -427,8 +424,7 @@
     def finish_second():
         normed_grad = total(p2, rx2, rp2, rm2)
         input_part = norm_back(normed_grad * gain[...].astype(F32), own_unit[...], own_scale[...])
-        out1[...] = (gc1[...].astype(F32) + input_part).astype(BF16)
-        keeps[3].start()
+        second_ref[...] = (gc1[...].astype(F32) + input_part).astype(BF16)
 
     task("prep", (), prepare)
 
@@ -465,21 +461,21 @@
         big, half, big, half, recv, recv, recv, recv, recv, recv,
         pltpu.VMEM((3, 2, 2, tok, HD), F32), pltpu.VMEM((2, 2, 2, tok, HD), F32), pltpu.VMEM((2, 2, 2, tok, 1), F32),
         pltpu.VMEM((2, 2, tok, tok), F32), pltpu.VMEM((2, tok, width), BF16), pltpu.VMEM((2, tok, width), BF16),
-        pltpu.VMEM((2, tok, 3 * width), BF16), pltpu.VMEM((1, D), BF16), rows, rows, pltpu.VMEM((R, D), F32), pltpu.VMEM((R, 1), F32),
+        pltpu.VMEM((2, tok, 3 * width), BF16), pltpu.VMEM((1, D), BF16), pltpu.VMEM((R, D), F32), pltpu.VMEM((R, 1), F32),
         pltpu.SemaphoreType.DMA((N_SHIFT + N_SEND,)), pltpu.SemaphoreType.DMA((N_RECV,)), pltpu.SemaphoreType.DMA((4,)),
-        pltpu.SemaphoreType.DMA((5,)), pltpu.SemaphoreType.DMA((4,)),
+        pltpu.SemaphoreType.DMA((5,)), pltpu.SemaphoreType.DMA((2,)),
     ]
     block = jax.ShapeDtypeStruct((R, D), BF16)
     out = jax.ShapeDtypeStruct((1, 2, R, D), BF16)
     anywhere = pl.BlockSpec(memory_space=pl.ANY)
     blocks = pl.pallas_call(
         functools.partial(kernel, n_section),
-        out_shape=(block,) * 4,
-        in_specs=[anywhere] * 7,
-        out_specs=[anywhere] * 4,
+        out_shape=(pltpu.VMEM((R, D), BF16),) * 4,
+        in_specs=[pl.BlockSpec(memory_space=pltpu.HBM)] * 7,
+        out_specs=[pl.BlockSpec(memory_space=pltpu.VMEM)] * 4,
         scratch_shapes=scratch,
         compiler_params=pltpu.CompilerParams(
-            collective_id=0, has_side_effects=True, vmem_limit_bytes=60 * 2**20
+            collective_id=0, has_side_effects=True, vmem_limit_bytes=56 * 2**20
         ),
         name="sublayer_back",
     )(handed_state, handed_grad, top_state, loss_grad, ln_gain, w_qkv, w_out)
@@ -487,22 +483,18 @@
     return pl.pallas_call(
         assemble,
         out_shape=(out, out),
-        in_specs=[anywhere] * 4,
-        out_specs=[anywhere] * 2,
-        scratch_shapes=[pltpu.VMEM((4, R, D), BF16), pltpu.SemaphoreType.DMA((4,)), pltpu.SemaphoreType.DMA((4,))],
+        in_specs=[pl.BlockSpec(memory_space=pltpu.VMEM)] * 4,
+        out_specs=[pl.BlockSpec(memory_space=pltpu.HBM)] * 2,
+        scratch_shapes=[pltpu.SemaphoreType.DMA((4,))],
         name="assemble",
-    )(*blocks)
-
-
-def assemble(first_ref, kept_c_ref, kept_g_ref, second_ref, rebuilt_ref, grads_ref, rows, in_sem, out_sem):
+    )(*[pltpu.with_memory_space_constraint(b, pltpu.VMEM) for b in blocks])
+
+
+def assemble(first_ref, kept_c_ref, kept_g_ref, second_ref, rebuilt_ref, grads_ref, sem):
     ins = (first_ref, kept_c_ref, kept_g_ref, second_ref)
     outs = (rebuilt_ref.at[0, 0], rebuilt_ref.at[0, 1], grads_ref.at[0, 0], grads_ref.at[0, 1])
-    loads = [pltpu.make_async_copy(src, rows.at[i], in_sem.at[i]) for i, src in enumerate(ins)]
-    stores = [pltpu.make_async_copy(rows.at[i], dst, out_sem.at[i]) for i, dst in enumerate(outs)]
-    for load in loads:
-        load.start()
-    for load, store in zip(loads, stores):
-        load.wait()
+    stores = [pltpu.make_async_copy(src, dst, sem.at[i]) for i, (src, dst) in enumerate(zip(ins, outs))]
+    for store in stores:
         store.start()
     for store in stores:
         store.wait()

time: 74.3 us -> 72.7 us (0.978)
  Pallas kernels: 72.1 us -> 70.5 us
    pallas_call x2, Pallas kernels: 72.1 us -> 70.5 us  [the longest x1 69.5 us: on_device(): pl.pallas_call(functools.partial(kernel, n_section), out_shape=(pltpu.VME...]
where the time goes in v3:
time: 72.7 us; the launch traced here: 71.3 us
  Pallas kernels  70.5 us (97%)
  between operations  0.8 us (1%)
    pallas_call x1, Pallas kernels, on_device(): pl.pallas_call(functools.partial(kernel, n_section), out_shape=(pltpu.VME...  69.5 us

profile of v3, /device:TPU:4, one launch (start us, length us, event | category | flops | bytes accessed | tf_op | source)
XLA Modules:
  0.0 71.3 jit_solution(10839359816759936314)
XLA Ops:
  0.6 69.5 %sublayer_back.1 = (bf16[32,4096]{1,0:T(8,128)(2,1)S(1)}, bf16[32,4096]{1,0:T(8,128)(2,1)S(1)}, bf16[32,4096]{1,0:T(8,128)(2,1)S(1)}, bf16[32,4096]{1,0:T(8,128)(2,1)S(1)}) custom-call(bf16[1,2,32,4096]{3,2,1,0:T(8,128)(2,1)} %state_ref.1, bf16[1,2,32,4096]{3,2,1,0:T(8,128)(2,1)} %grad_ref.1, bf16[2,32,4096]{2,1,0:T(8,128)(2,1)} %top_ref.1, ...), custom_call_target="tpu_custom_call" | custom-call | tf_op jit(solution)/shard_map/sublayer_back/pallas_call | solution.py:471
  70.1 1.0 %assemble.1 = (bf16[1,2,32,4096]{3,2,1,0:T(8,128)(2,1)}, bf16[1,2,32,4096]{3,2,1,0:T(8,128)(2,1)}) custom-call(bf16[32,4096]{1,0:T(8,128)(2,1)S(1)} %get-tuple-element.6.first_ref, bf16[32,4096]{1,0:T(8,128)(2,1)S(1)} %get-tuple-element.7.kept_c_ref, bf16[32,4096]{1,0:T(8,128)(2,1)S(1)} %get-tuple-element.8.kept_g_ref, ...), custom_call_target="tpu_custom_call" | custom-call | tf_op jit(solution)/shard_map/assemble/pallas_call | solution.py:483

commit v4 on v3

--- a/solution.py
+++ b/solution.py
@@ -12,14 +12,14 @@
 F32 = jnp.float32
 BF16 = jnp.bfloat16
 R = 32
-N_SHIFT, N_SEND, N_RECV = 10, 40, 93
+N_SHIFT, N_SEND, N_RECV = 10, 32, 93
 ORDER = (
     0, 1, 2, 3, 4, 5, 6, 7, 8, 12, 17, 16, 20, 21, 10, 11, 28, 72, 9, 14, 23, 73, 37, 24, 13, 38, 36, 40, 30, 76,
-    15, 32, 80, 41, 164, 18, 64, 77, 19, 25, 29, 74, 81, 26, 44, 43, 75, 22, 39, 46, 47, 42, 31, 78, 33, 82, 45, 53,
-    57, 79, 34, 88, 27, 48, 56, 60, 89, 49, 51, 59, 66, 68, 92, 50, 52, 65, 83, 117, 84, 54, 55, 85, 94, 96, 98,
-    100, 35, 116, 86, 123, 122, 87, 102, 58, 61, 62, 67, 124, 125, 103, 63, 69, 70, 118, 106, 130, 131, 90, 120,
-    108, 91, 110, 112, 114, 119, 126, 127, 93, 71, 121, 134, 128, 129, 95, 97, 148, 145, 99, 101, 139, 104, 132,
-    133, 105, 140, 107, 136, 135, 137, 138, 109, 111, 141, 146, 147, 143, 113, 115, 150, 153, 142, 152, 149, 165,
+    15, 32, 80, 164, 18, 41, 64, 77, 25, 29, 74, 19, 81, 26, 22, 75, 43, 44, 39, 46, 47, 42, 31, 78, 33, 82, 45, 53,
+    57, 79, 34, 88, 27, 48, 56, 60, 89, 49, 51, 59, 66, 68, 92, 50, 52, 65, 83, 84, 117, 85, 94, 55, 54, 96, 98,
+    100, 116, 35, 86, 123, 122, 87, 102, 58, 61, 62, 67, 124, 103, 63, 69, 70, 118, 125, 106, 130, 131, 90, 108,
+    120, 91, 110, 112, 114, 126, 127, 93, 71, 119, 134, 128, 129, 95, 121, 97, 99, 148, 101, 145, 104, 139, 105,
+    132, 133, 107, 140, 136, 135, 137, 138, 109, 111, 141, 146, 147, 113, 115, 143, 150, 153, 142, 152, 149, 165,
     144, 157, 154, 151, 163, 156, 159, 155, 158, 161, 160, 162, 166,
 )
 

time: 72.7 us -> 72.5 us (level)
  no operation moved by 1% of the time
where the time goes in v4:
time: 72.5 us; the launch traced here: 71.2 us
  Pallas kernels  70.4 us (97%)
  between operations  0.8 us (1%)
    pallas_call x1, Pallas kernels, on_device(): pl.pallas_call(functools.partial(kernel, n_section), out_shape=(pltpu.VME...  69.4 us

profile of v4, /device:TPU:4, one launch (start us, length us, event | category | flops | bytes accessed | tf_op | source)
XLA Modules:
  0.0 71.2 jit_solution(10801036572408748183)
XLA Ops:
  0.6 69.4 %sublayer_back.1 = (bf16[32,4096]{1,0:T(8,128)(2,1)S(1)}, bf16[32,4096]{1,0:T(8,128)(2,1)S(1)}, bf16[32,4096]{1,0:T(8,128)(2,1)S(1)}, bf16[32,4096]{1,0:T(8,128)(2,1)S(1)}) custom-call(bf16[1,2,32,4096]{3,2,1,0:T(8,128)(2,1)} %state_ref.1, bf16[1,2,32,4096]{3,2,1,0:T(8,128)(2,1)} %grad_ref.1, bf16[2,32,4096]{2,1,0:T(8,128)(2,1)} %top_ref.1, ...), custom_call_target="tpu_custom_call" | custom-call | tf_op jit(solution)/shard_map/sublayer_back/pallas_call | solution.py:471
  70.1 1.0 %assemble.1 = (bf16[1,2,32,4096]{3,2,1,0:T(8,128)(2,1)}, bf16[1,2,32,4096]{3,2,1,0:T(8,128)(2,1)}) custom-call(bf16[32,4096]{1,0:T(8,128)(2,1)S(1)} %get-tuple-element.6.first_ref, bf16[32,4096]{1,0:T(8,128)(2,1)S(1)} %get-tuple-element.7.kept_c_ref, bf16[32,4096]{1,0:T(8,128)(2,1)S(1)} %get-tuple-element.8.kept_g_ref, ...), custom_call_target="tpu_custom_call" | custom-call | tf_op jit(solution)/shard_map/assemble/pallas_call | solution.py:483
